TPU v7x, 512 devices: a whole 4x4x16 slice. The times are simulated.
512 devices in a mesh: prow: 16 (over z), pcol: 32 (over y, x, core).
Axes of the slice: x: 4, y: 4, z: 16, core: 2. Of those that a mesh axis runs over, the one named last changes fastest.
Arguments:
- diag_inverse: float32 [8, 2048, 2048], P(None, 'pcol', 'prow'), as said below
- off_blocks: bfloat16 [28, 2048, 2048], P(None, 'pcol', 'prow'), may hold values from -0.046875 to 0.046875
- low_factor: bfloat16 [49152, 8, 2048], P('pcol', None, 'prow'), may hold values from -0.09375 to 0.09375
- rhs_top: float32 [8, 2048, 256], P(None, 'pcol'), may hold values from -6 to 6
- rhs_low: float32 [49152, 256], P(('pcol', 'prow')), may hold values from -6 to 6
Outputs:
- solved: float32 [8, 2048, 256], P(None, ('prow', 'pcol'))
- remaining: float32 [49152, 256], P(('pcol', 'prow'))
Inputs may be any that keep to these rules, and one draw needn't show every extreme that they name: diag_inverse[k, c, r] is entry (r, c) of the inverse of the k-th diagonal factor block: lower triangular in (r, c), zero where c > r, diagonal between 1 and 2.
All inputs are finite; a program needn't handle non-finite values.
Results may differ from a plain program's by a relative error of at most 0.0059.
Values sent between devices are 32-bit elements; how exact they have to be, the bound alone decides.
A program may use at most 64 MiB of HBM per device.

v0:
```python
import jax
import jax.numpy as jnp
from jax import lax
from jax.sharding import PartitionSpec as P


def pair_slot(target, source):
    return target * (target - 1) // 2 + source


def on_device(diag_inverse, off_blocks, low_factor, rhs_top, rhs_low):
    panels = diag_inverse.shape[0]
    low_rows = low_factor.shape[0]
    sides = rhs_top.shape[2]
    pending = [rhs_top[panel] for panel in range(panels)]
    trailing_acc = jnp.zeros((low_rows, sides), jnp.float32)
    solutions = []
    rounded = []
    for panel in range(panels):
        current = pending[panel]
        share_x = jnp.einsum(
            "cr,cq->rq", diag_inverse[panel], current, precision=lax.Precision.HIGHEST
        )
        solution = lax.psum(share_x, "pcol")
        packed = solution.astype(jnp.bfloat16)
        solutions.append(solution)
        rounded.append(packed)
        later_panels = list(range(panel + 1, panels))
        if later_panels:
            products = jnp.stack(
                [
                    jnp.dot(
                        off_blocks[pair_slot(target, panel)],
                        packed,
                        preferred_element_type=jnp.float32,
                    )
                    for target in later_panels
                ]
            )
            summed = lax.psum(products, "prow")
            for position, target in enumerate(later_panels):
                pending[target] = pending[target] - summed[position]
        trailing_acc = trailing_acc + jnp.dot(
            low_factor[:, panel, :], packed, preferred_element_type=jnp.float32
        )
    reduced = lax.psum_scatter(trailing_acc, "prow", scatter_dimension=0, tiled=True)
    remaining = rhs_low - reduced
    solved_all = jnp.stack(solutions)
    slice_rows = solved_all.shape[1] // lax.axis_size("pcol")
    first_row = lax.axis_index("pcol") * slice_rows
    solved = lax.dynamic_slice_in_dim(solved_all, first_row, slice_rows, 1)
    return (solved, remaining)


def solution(mesh):
    placed = (
        P(None, "pcol", "prow"),
        P(None, "pcol", "prow"),
        P("pcol", None, "prow"),
        P(None, "pcol", None),
        P(("pcol", "prow"), None),
    )
    return jax.shard_map(
        on_device,
        mesh=mesh,
        in_specs=placed,
        out_specs=(P(None, ("prow", "pcol"), None), P(("pcol", "prow"), None)),
        check_vma=False,
    )
```

profile of v0, /device:TPU:6, one launch (start us, length us, event | category | flops | bytes accessed | tf_op | source)
XLA Modules:
  0.0 2125.3 jit_solution(15491402596146420548)
XLA Ops:
  9.1 137.8 %all-reduce.16.cloned.1.call-done = f32[128,256]{1,0:T(8,128)} async-done(((f32[128,256]{1,0:T(8,128)}), f32[128,256]{1,0:T(8,128)}) %all-reduce.16.cloned.1.call-update) | async-done | bytes 131088 | tf_op jit(solution)/shard_map/psum | solution.py:24
  154.7 135.8 %all-reduce.18.cloned.1.call-done = f32[7,64,256]{2,1,0:T(8,128)} async-done(((f32[7,64,256]{2,1,0:T(8,128)}), f32[7,64,256]{2,1,0:T(8,128)}) %all-reduce.18.cloned.1.call-update) | async-done | bytes 458768 | tf_op jit(solution)/shard_map/psum | solution.py:40
  292.4 128.9 %all-reduce.20.cloned.1.call-done = f32[128,256]{1,0:T(8,128)} async-done(((f32[128,256]{1,0:T(8,128)}), f32[128,256]{1,0:T(8,128)}) %all-reduce.20.cloned.1.call-update) | async-done | bytes 131088 | tf_op jit(solution)/shard_map/psum | solution.py:24
  428.1 135.4 %all-reduce.22.cloned.1.call-done = f32[6,64,256]{2,1,0:T(8,128)} async-done(((f32[6,64,256]{2,1,0:T(8,128)}), f32[6,64,256]{2,1,0:T(8,128)}) %all-reduce.22.cloned.1.call-update) | async-done | bytes 393232 | tf_op jit(solution)/shard_map/psum | solution.py:40
  565.5 129.2 %all-reduce.24.cloned.1.call-done = f32[128,256]{1,0:T(8,128)} async-done(((f32[128,256]{1,0:T(8,128)}), f32[128,256]{1,0:T(8,128)}) %all-reduce.24.cloned.1.call-update) | async-done | bytes 131088 | tf_op jit(solution)/shard_map/psum | solution.py:24
  703.2 135.1 %all-reduce.26.cloned.1.call-done = f32[5,64,256]{2,1,0:T(8,128)} async-done(((f32[5,64,256]{2,1,0:T(8,128)}), f32[5,64,256]{2,1,0:T(8,128)}) %all-reduce.26.cloned.1.call-update) | async-done | bytes 327696 | tf_op jit(solution)/shard_map/psum | solution.py:40
  838.4 1.9 convolution_bitcast_fusion.4
  840.3 129.0 %all-reduce.28.cloned.1.call-done = f32[128,256]{1,0:T(8,128)} async-done(((f32[128,256]{1,0:T(8,128)}), f32[128,256]{1,0:T(8,128)}) %all-reduce.28.cloned.1.call-update) | async-done | bytes 131088 | tf_op jit(solution)/shard_map/psum | solution.py:24
  974.4 6.4 fusion.123
  980.9 128.2 %all-reduce.30.cloned.1.call-done = f32[4,64,256]{2,1,0:T(8,128)} async-done(((f32[4,64,256]{2,1,0:T(8,128)}), f32[4,64,256]{2,1,0:T(8,128)}) %all-reduce.30.cloned.1.call-update) | async-done | bytes 262160 | tf_op jit(solution)/shard_map/psum | solution.py:40
  1109.1 1.9 convolution_bitcast_fusion.3
  1112.6 127.9 %all-reduce.32.cloned.1.call-done = f32[128,256]{1,0:T(8,128)} async-done(((f32[128,256]{1,0:T(8,128)}), f32[128,256]{1,0:T(8,128)}) %all-reduce.32.cloned.1.call-update) | async-done | bytes 131088 | tf_op jit(solution)/shard_map/psum | solution.py:24
  1246.3 132.8 %all-reduce.34.cloned.1.call-done = f32[3,64,256]{2,1,0:T(8,128)} async-done(((f32[3,64,256]{2,1,0:T(8,128)}), f32[3,64,256]{2,1,0:T(8,128)}) %all-reduce.34.cloned.1.call-update) | async-done | bytes 196624 | tf_op jit(solution)/shard_map/psum | solution.py:40
  1379.0 2.0 convolution_bitcast_fusion.2
  1382.6 126.7 %all-reduce.36.cloned.1.call-done = f32[128,256]{1,0:T(8,128)} async-done(((f32[128,256]{1,0:T(8,128)}), f32[128,256]{1,0:T(8,128)}) %all-reduce.36.cloned.1.call-update) | async-done | bytes 131088 | tf_op jit(solution)/shard_map/psum | solution.py:24
  1513.7 132.0 %all-reduce.38.cloned.1.call-done = f32[2,64,256]{2,1,0:T(8,128)} async-done(((f32[2,64,256]{2,1,0:T(8,128)}), f32[2,64,256]{2,1,0:T(8,128)}) %all-reduce.38.cloned.1.call-update) | async-done | bytes 131088 | tf_op jit(solution)/shard_map/psum | solution.py:40
  1645.7 2.0 convolution_bitcast_fusion.1
  1647.8 2.7 convolution_add_fusion.3
  1650.5 126.6 %all-reduce.40.cloned.1.call-done = f32[128,256]{1,0:T(8,128)} async-done(((f32[128,256]{1,0:T(8,128)}), f32[128,256]{1,0:T(8,128)}) %all-reduce.40.cloned.1.call-update) | async-done | bytes 131088 | tf_op jit(solution)/shard_map/psum | solution.py:24
  1779.0 2.1 convolution_add_fusion.2
  1781.0 131.7 %all-reduce.42.cloned.1.call-done = f32[1,64,256]{2,1,0:T(8,128)} async-done(((f32[1,64,256]{2,1,0:T(8,128)}), f32[1,64,256]{2,1,0:T(8,128)}) %all-reduce.42.cloned.1.call-update) | async-done | bytes 65552 | tf_op jit(solution)/shard_map/psum | solution.py:40
  1912.7 2.0 convolution_bitcast_fusion
  1916.3 126.5 %all-reduce.44.cloned.1.call-done = f32[128,256]{1,0:T(8,128)} async-done(((f32[128,256]{1,0:T(8,128)}), f32[128,256]{1,0:T(8,128)}) %all-reduce.44.cloned.1.call-update) | async-done | bytes 131088 | tf_op jit(solution)/shard_map/psum | solution.py:24
  2048.0 69.0 %reduce-scatter.4.cloned.1.call-done = f32[96,256]{1,0:T(8,128)} async-done(((f32[1536,256]{1,0:T(8,128)}), f32[96,256]{1,0:T(8,128)}) %reduce-scatter.4.cloned.1.call-update) | async-done | bytes 98320
  (117 shorter events, 57.4 us)
Async XLA Ops:
  7.2 139.8 %all-reduce.16.cloned.1.call-start = ((), (), s32[]{:S(2)}) async-start(), calls=%async_computation.1 | async-start | bytes 262144 | tf_op jit(solution)/shard_map/psum | solution.py:24
  9.1 281.4 %all-reduce.18.cloned.1.call-start = ((), (), s32[]{:S(2)}) async-start(), calls=%async_computation.2 | async-start | bytes 917504 | tf_op jit(solution)/shard_map/psum | solution.py:40
  154.6 266.6 %all-reduce.20.cloned.1.call-start = ((), (), s32[]{:S(2)}) async-start(), calls=%async_computation.3 | async-start | bytes 262144 | tf_op jit(solution)/shard_map/psum | solution.py:24
  292.3 271.2 %all-reduce.22.cloned.1.call-start = ((), (), s32[]{:S(2)}) async-start(), calls=%async_computation.4 | async-start | bytes 786432 | tf_op jit(solution)/shard_map/psum | solution.py:40
  428.1 266.6 %all-reduce.24.cloned.1.call-start = ((), (), s32[]{:S(2)}) async-start(), calls=%async_computation.5 | async-start | bytes 262144 | tf_op jit(solution)/shard_map/psum | solution.py:24
  565.4 272.9 %all-reduce.26.cloned.1.call-start = ((), (), s32[]{:S(2)}) async-start(), calls=%async_computation.6 | async-start | bytes 655360 | tf_op jit(solution)/shard_map/psum | solution.py:40
  695.6 278.8 %copy-start = (bf16[1536,8,128]{2,1,0:T(8,128)(2,1)S(1)}, bf16[1536,8,128]{2,1,0:T(8,128)(2,1)}, u32[]{:S(2)}) copy-start(bf16[1536,8,128]{2,1,0:T(8,128)(2,1)} %param.7) | copy-start | bytes 9437188
  703.2 266.1 %all-reduce.28.cloned.1.call-start = ((), (), s32[]{:S(2)}) async-start(), calls=%async_computation.7 | async-start | bytes 262144 | tf_op jit(solution)/shard_map/psum | solution.py:24
  840.3 268.8 %all-reduce.30.cloned.1.call-start = ((), (), s32[]{:S(2)}) async-start(), calls=%async_computation.8 | async-start | bytes 524288 | tf_op jit(solution)/shard_map/psum | solution.py:40
  974.4 266.1 %all-reduce.32.cloned.1.call-start = ((), (), s32[]{:S(2)}) async-start(), calls=%async_computation.9 | async-start | bytes 262144 | tf_op jit(solution)/shard_map/psum | solution.py:24
  1111.0 268.0 %all-reduce.34.cloned.1.call-start = ((), (), s32[]{:S(2)}) async-start(), calls=%async_computation.10 | async-start | bytes 393216 | tf_op jit(solution)/shard_map/psum | solution.py:40
  1244.7 264.6 %all-reduce.36.cloned.1.call-start = ((), (), s32[]{:S(2)}) async-start(), calls=%async_computation.11 | async-start | bytes 262144 | tf_op jit(solution)/shard_map/psum | solution.py:24
  1381.0 264.7 %all-reduce.38.cloned.1.call-start = ((), (), s32[]{:S(2)}) async-start(), calls=%async_computation.12 | async-start | bytes 262144 | tf_op jit(solution)/shard_map/psum | solution.py:40
  1512.1 265.1 %all-reduce.40.cloned.1.call-start = ((), (), s32[]{:S(2)}) async-start(), calls=%async_computation.13 | async-start | bytes 262144 | tf_op jit(solution)/shard_map/psum | solution.py:24
  1647.7 265.0 %all-reduce.42.cloned.1.call-start = ((), (), s32[]{:S(2)}) async-start(), calls=%async_computation.14 | async-start | bytes 131072 | tf_op jit(solution)/shard_map/psum | solution.py:40
  1647.8 131.1 %copy-start.1 = (f32[128,256]{1,0:T(8,128)S(1)}, f32[128,256]{1,0:T(8,128)}, u32[]{:S(2)}) copy-start(f32[128,256]{1,0:T(8,128)} %all-reduce.36.cloned.1.call-done) | copy-start | bytes 393220
  1778.9 263.9 %all-reduce.44.cloned.1.call-start = ((), (), s32[]{:S(2)}) async-start(), calls=%async_computation.15 | async-start | bytes 262144 | tf_op jit(solution)/shard_map/psum | solution.py:24
  1778.9 133.8 %copy-start.11 = (f32[2,64,256]{2,1,0:T(8,128)S(1)}, f32[2,64,256]{2,1,0:T(8,128)}, u32[]{:S(2)}) copy-start(f32[2,64,256]{2,1,0:T(8,128)} %all-reduce.38.cloned.1.call-done) | copy-start | bytes 393220
  1779.0 135.8 %copy-start.2 = (f32[128,256]{1,0:T(8,128)S(1)}, f32[128,256]{1,0:T(8,128)}, u32[]{:S(2)}) copy-start(f32[128,256]{1,0:T(8,128)} %all-reduce.40.cloned.1.call-done) | copy-start | bytes 393220
  1914.7 202.3 %reduce-scatter.4.cloned.1.call-start = ((), (), s32[]{:S(2)}) async-start(), calls=%async_computation.16 | async-start | bytes 1671168
  2046.1 1.1 copy-start.8
  2046.1 1.1 copy-start.9
  2046.1 1.2 copy-start.10
  2046.1 1.2 copy-start.5
  (5 other events, 4.4 us)
Sparse Core Ops, SparseCore 0:
  11.2 135.7 all-reduce.15
  154.8 135.6 all-reduce.17
  293.7 127.5 all-reduce.19
  428.2 135.3 all-reduce.21
  566.6 128.0 all-reduce.23
  703.3 135.0 all-reduce.25
  841.6 127.6 all-reduce.27
  974.5 134.5 all-reduce.29
  1112.3 128.1 all-reduce.31
  1244.8 134.2 all-reduce.33
  1382.3 126.9 all-reduce.35
  1512.2 133.4 all-reduce.37
  1648.9 128.2 all-reduce.39
  1780.0 132.6 all-reduce.41
  1915.8 127.0 all-reduce.43
  2046.2 70.7 reduce-scatter.3
where the time goes:
time: 2130 us
  waiting for transfers between devices  2030 us (95%)
  matrix products  57.7 us (3%)
    psum x8, waiting for transfers between devices, on_device(): solution = lax.psum(share_x, 'pcol')  1030 us
    psum x7, waiting for transfers between devices, on_device(): summed = lax.psum(products, 'prow')  931 us
    unnamed x17, waiting for transfers between devices  69.3 us
  transfers between devices with their start and end apart: 16, of which 16 were waited for; matrix products, arithmetic and copies ran while one was open for 1% of the time, Pallas kernels for 0%

commit v1 on v0

v1 whole, which is shorter than its diff:
```python
import functools

import jax
import jax.numpy as jnp
from jax import lax
from jax.experimental import pallas as pl
from jax.experimental.pallas import tpu as pltpu
from jax.sharding import PartitionSpec as P

MESH = pl.DeviceIdType.MESH
F32 = jnp.float32
BF16 = jnp.bfloat16
PANELS = 8
NZ = 16
NP = 32
COLS = 128
ROWS = 64
SIDES = 256
LOW = 1536
OWN = LOW // NZ
SUB = 2
PIECE = OWN // SUB
DOWN = NZ // 2
UP = NZ - 1 - DOWN


def plane_offsets():
    offsets = [(dy, dx, dc) for dy in range(4) for dx in range(4) for dc in range(2)]
    offsets.remove((0, 0, 0))
    ring = (0, 1, 2, 1)
    return sorted(offsets, key=lambda o: -(ring[o[0]] + ring[o[1]] + 0.5 * o[2]))


def ring_offsets():
    return sorted(range(1, NZ), key=lambda d: -min(d, NZ - d))


def await_bytes(view, sem):
    pltpu.make_async_copy(view, view, sem).wait()


def tiles_of(value):
    rows = value.shape[0]
    left = value[:, :128].reshape(rows // 8, 8, 128)
    right = value[:, 128:].reshape(rows // 8, 8, 128)
    return left, right


def whole_of(tiles):
    count = tiles.shape[0] // 2
    left = tiles[:count].reshape(count * 8, 128)
    right = tiles[count:].reshape(count * 8, 128)
    return jnp.concatenate([left, right], axis=1)


def kernel(
    d_ref, o_ref, low_ref, top_ref, rhs_ref, solved_ref, out_ref,
    stacked, pending, share, share_in, x_tiles, x_low, sums, sums_in, cur_tiles,
    low_in, low_flat, loose, down_out, down_in, up_out, up_in,
    low_sem, share_sem, x_sem, sums_sem, cur_sem, down_sem, up_sem,
    share_send, x_send, sums_send, cur_send, down_send, up_send,
):
    i = lax.axis_index("prow")
    j = lax.axis_index("pcol")
    y, x, core = j // 8, (j // 2) % 4, j % 2

    def plane_peer(offset):
        dy, dx, dc = offset
        return ((y + dy) % 4) * 8 + ((x + dx) % 4) * 2 + (core + dc) % 2

    load_low = pltpu.make_async_copy(low_ref, low_in, low_sem)
    load_low.start()

    barrier = pltpu.get_barrier_semaphore()
    for offset in plane_offsets():
        pl.semaphore_signal(
            barrier, inc=1, device_id=(i, plane_peer(offset)), device_id_type=MESH
        )
    for d in ring_offsets():
        pl.semaphore_signal(
            barrier, inc=1, device_id=((i + d) % NZ, j), device_id_type=MESH
        )

    for k in range(PANELS):
        d = d_ref[k]
        hi = d.astype(BF16).astype(F32)
        lo = d - hi
        terms = jnp.concatenate([hi, hi, lo, lo], axis=0)
        stacked[k] = terms.T.astype(BF16)
    pending[...] = jnp.zeros_like(pending)
    pl.semaphore_wait(barrier, NP - 1 + NZ - 1)

    def diagonal(k, current):
        hi = current.astype(BF16)
        lo = (current - hi.astype(F32)).astype(BF16)
        terms = jnp.concatenate([hi, lo, hi, lo], axis=0)
        product = jnp.dot(stacked[k], terms, preferred_element_type=F32)
        left, right = tiles_of(product)
        share[k, : NP // 2] = left
        share[k, NP // 2 :] = right
        for offset in plane_offsets():
            peer = plane_peer(offset)
            pltpu.make_async_remote_copy(
                src_ref=share.at[k, peer], dst_ref=share_in.at[k, j],
                send_sem=share_send, recv_sem=share_sem.at[k],
                device_id=(i, peer), device_id_type=MESH,
            ).start()
        share_in[k, j] = share[k, j]

    def solve(k):
        await_bytes(share_in.at[k, pl.ds(0, NP - 1)], share_sem.at[k])
        x_tiles[k, j] = jnp.sum(share_in[k], axis=0)
        for offset in plane_offsets():
            peer = plane_peer(offset)
            pltpu.make_async_remote_copy(
                src_ref=x_tiles.at[k, j], dst_ref=x_tiles.at[k, j],
                send_sem=x_send, recv_sem=x_sem.at[k],
                device_id=(i, peer), device_id_type=MESH,
            ).start()

    def gathered(k):
        await_bytes(x_tiles.at[k, pl.ds(0, NP - 1)], x_sem.at[k])
        packed = whole_of(x_tiles[k]).astype(BF16)
        x_low[pl.ds(pl.multiple_of(k * COLS, COLS), COLS), :] = packed
        return packed

    def solved_rows(k):
        half = j // 2
        for c in range(2):
            tile = x_tiles[k, c * (NP // 2) + half]
            solved_ref[k, :, c * 128 : (c + 1) * 128] = jnp.where(
                j % 2 == 0, tile[:4], tile[4:]
            )

    def flatten(b):
        rows = pl.ds(pl.multiple_of(b * OWN, OWN), OWN)
        loose[...] = low_in[rows].astype(F32).reshape(OWN * PANELS, COLS)
        for k in range(PANELS):
            low_flat[rows, k * COLS : (k + 1) * COLS] = loose[
                pl.ds(k, OWN, stride=PANELS), :
            ].astype(BF16)

    diagonal(0, top_ref[0])
    load_low.wait()

    def panel_step(k, carry):
        flatten(2 * k)
        solve(k)
        flatten(2 * k + 1)
        packed = gathered(k)
        t = k + 1
        slot = t * (t - 1) // 2 + k
        update = pending[t] + jnp.dot(o_ref[slot], packed, preferred_element_type=F32)
        left, right = tiles_of(update)
        sums[t, : NZ // 2] = left
        sums[t, NZ // 2 :] = right
        for d in ring_offsets():
            peer = (i + d) % NZ
            pltpu.make_async_remote_copy(
                src_ref=sums.at[t, peer], dst_ref=sums_in.at[t, i],
                send_sem=sums_send, recv_sem=sums_sem.at[t],
                device_id=(peer, j), device_id_type=MESH,
            ).start()
        sums_in[t, i] = sums[t, i]

        def later(u, c):
            other = u * (u - 1) // 2 + k
            pending[u] = pending[u] + jnp.dot(
                o_ref[other], packed, preferred_element_type=F32
            )
            return c

        lax.fori_loop(k + 2, PANELS, later, 0)
        solved_rows(k)

        await_bytes(sums_in.at[t, pl.ds(0, NZ - 1)], sums_sem.at[t])
        row = pl.multiple_of((i % 8) * 8, 8)
        rhs = jnp.where(
            i < 8, top_ref[t, pl.ds(row, 8), :128], top_ref[t, pl.ds(row, 8), 128:]
        )
        cur_tiles[t, i] = rhs - jnp.sum(sums_in[t], axis=0)
        for d in ring_offsets():
            peer = (i + d) % NZ
            pltpu.make_async_remote_copy(
                src_ref=cur_tiles.at[t, i], dst_ref=cur_tiles.at[t, i],
                send_sem=cur_send, recv_sem=cur_sem.at[t],
                device_id=(peer, j), device_id_type=MESH,
            ).start()
        await_bytes(cur_tiles.at[t, pl.ds(0, NZ - 1)], cur_sem.at[t])
        diagonal(t, whole_of(cur_tiles[t]))
        return carry

    lax.fori_loop(0, PANELS - 1, panel_step, 0)
    last = PANELS - 1
    flatten(2 * last)
    solve(last)
    flatten(2 * last + 1)
    gathered(last)

    def term(owner):
        rows = pl.ds(pl.multiple_of(owner * OWN, OWN), OWN)
        return jnp.dot(low_flat[rows, :], x_low[...], preferred_element_type=F32)

    below, above = (i + NZ - 1) % NZ, (i + 1) % NZ

    def hop(step, owner, outgoing, incoming, send, recv, peer):
        own = term(owner)
        for q in range(SUB):
            part = pl.ds(q * PIECE, PIECE)
            value = own[q * PIECE : (q + 1) * PIECE]
            if step:
                await_bytes(incoming.at[step - 1, part], recv.at[step - 1, q])
                value = value + incoming[step - 1, part, :]
            outgoing[step, part, :] = value
            pltpu.make_async_remote_copy(
                src_ref=outgoing.at[step, part], dst_ref=incoming.at[step, part],
                send_sem=send, recv_sem=recv.at[step, q],
                device_id=(peer, j), device_id_type=MESH,
            ).start()

    for step in range(DOWN):
        hop(step, (i + DOWN + step) % NZ, down_out, down_in, down_send, down_sem, below)
        if step < UP:
            hop(step, (i + UP - step) % NZ, up_out, up_in, up_send, up_sem, above)
    solved_rows(last)
    own = term(i)
    for q in range(SUB):
        part = pl.ds(q * PIECE, PIECE)
        await_bytes(up_in.at[UP - 1, part], up_sem.at[UP - 1, q])
        await_bytes(down_in.at[DOWN - 1, part], down_sem.at[DOWN - 1, q])
        out_ref[part, :] = rhs_ref[part, :] - (
            own[q * PIECE : (q + 1) * PIECE]
            + up_in[UP - 1, part, :]
            + down_in[DOWN - 1, part, :]
        )

    await_bytes(share_in.at[:, pl.ds(0, NP - 1)], share_send)
    await_bytes(x_tiles.at[:, pl.ds(0, NP - 1)], x_send)
    await_bytes(sums_in.at[pl.ds(1, PANELS - 1), pl.ds(0, NZ - 1)], sums_send)
    await_bytes(cur_tiles.at[pl.ds(1, PANELS - 1), pl.ds(0, NZ - 1)], cur_send)
    await_bytes(down_in, down_send)
    await_bytes(up_in, up_send)


def on_device(diag_inverse, off_blocks, low_factor, rhs_top, rhs_low):
    vmem = pl.BlockSpec(memory_space=pltpu.VMEM)
    dma = pltpu.SemaphoreType.DMA
    return pl.pallas_call(
        kernel,
        out_shape=(
            jax.ShapeDtypeStruct((PANELS, ROWS // NZ, SIDES), F32),
            jax.ShapeDtypeStruct((OWN, SIDES), F32),
        ),
        in_specs=[vmem, vmem, pl.BlockSpec(memory_space=pl.ANY), vmem, vmem],
        out_specs=(vmem, vmem),
        scratch_shapes=[
            pltpu.VMEM((PANELS, COLS, 4 * ROWS), BF16),
            pltpu.VMEM((PANELS, ROWS, SIDES), F32),
            pltpu.VMEM((PANELS, NP, 8, 128), F32),
            pltpu.VMEM((PANELS, NP, 8, 128), F32),
            pltpu.VMEM((PANELS, NP, 8, 128), F32),
            pltpu.VMEM((PANELS * COLS, SIDES), BF16),
            pltpu.VMEM((PANELS, NZ, 8, 128), F32),
            pltpu.VMEM((PANELS, NZ, 8, 128), F32),
            pltpu.VMEM((PANELS, NZ, 8, 128), F32),
            pltpu.VMEM((LOW, PANELS, COLS), BF16),
            pltpu.VMEM((LOW, PANELS * COLS), BF16),
            pltpu.VMEM((OWN * PANELS, COLS), F32),
            pltpu.VMEM((DOWN, OWN, SIDES), F32),
            pltpu.VMEM((DOWN, OWN, SIDES), F32),
            pltpu.VMEM((UP, OWN, SIDES), F32),
            pltpu.VMEM((UP, OWN, SIDES), F32),
            dma,
            dma((PANELS,)), dma((PANELS,)), dma((PANELS,)), dma((PANELS,)),
            dma((DOWN, SUB)), dma((UP, SUB)),
            dma, dma, dma, dma, dma, dma,
        ],
        compiler_params=pltpu.CompilerParams(
            collective_id=0, has_side_effects=True, vmem_limit_bytes=48 * 2**20
        ),
    )(diag_inverse, off_blocks, low_factor, rhs_top, rhs_low)


def solution(mesh):
    placed = (
        P(None, "pcol", "prow"),
        P(None, "pcol", "prow"),
        P("pcol", None, "prow"),
        P(None, "pcol", None),
        P(("pcol", "prow"), None),
    )
    return jax.shard_map(
        on_device,
        mesh=mesh,
        in_specs=placed,
        out_specs=(P(None, ("prow", "pcol"), None), P(("pcol", "prow"), None)),
        check_vma=False,
    )
```

time: 2130 us -> 231 us (0.11)
  waiting for transfers between devices: 2030 us -> 0 us
  Pallas kernels: 0 us -> 222 us
  matrix products: 57.7 us -> 0 us
    psum x15 -> x0, waiting for transfers between devices: 1960 us -> none  [the longest x8 1030 us: on_device(): solution = lax.psum(share_x, 'pcol')]
    pallas_call x0 -> x1, Pallas kernels: none -> 222 us  [on_device(): pl.pallas_call(kernel, out_shape=(jax.ShapeDtypeStruct((PANELS, ROWS // N...]
    unnamed x17 -> x0, waiting for transfers between devices: 69.3 us -> none
    dot_general x44 -> x0, matrix products: 57.7 us -> none  [the longest x28 28.4 us: on_device(): jnp.dot(off_blocks[pair_slot(target, panel)], packed, preferred_element_t...]
  transfers between devices with their start and end apart: 16 -> 0, of which waited for: 16 -> 0; matrix products, arithmetic and copies ran while one was open for 1% -> 0% of each run, Pallas kernels for 0% -> 0%
where the time goes in v1:
time: 231 us; the launch traced here: 230 us
  Pallas kernels  222 us (96%)
  local copies, waits for them, and re-layouts  7.04 us (3%)
    pallas_call x1, Pallas kernels, on_device(): pl.pallas_call(kernel, out_shape=(jax.ShapeDtypeStruct((PANELS, ROWS // N...  222 us
    unnamed x12, local copies, waits for them, and re-layouts  7.04 us

profile of v1, /device:TPU:6, one launch (start us, length us, event | category | flops | bytes accessed | tf_op | source)
XLA Modules:
  0.0 230.2 jit_solution(15439575362894485201)
XLA Ops:
  0.6 0.0 copy-start
  0.6 1.9 copy-done
  2.5 0.0 copy-start.1
  2.5 1.0 copy-done.1
  3.6 0.0 copy-start.2
  3.6 1.0 copy-done.2
  4.6 0.0 copy-start.3
  4.6 0.9 copy-done.3
  5.5 0.0 copy-start.4
  5.5 0.9 copy-done.4
  6.4 222.5 %shard_map.68 = (f32[8,4,256]{2,1,0:T(4,128)S(1)}, f32[96,256]{1,0:T(8,128)S(1)}) custom-call(f32[8,64,128]{2,1,0:T(8,128)S(1)} %copy-done.3, bf16[28,64,128]{2,1,0:T(8,128)(2,1)S(1)} %copy-done.2, bf16[1536,8,128]{2,1,0:T(8,128)(2,1)S(1)} %copy-done, f32[8,64,256]{2,1,0:T(8,128)S(1)} %copy-done.1, f32[96,256]{1,0:T(8,128)S(1)} %copy-done.4), custom_call_target="tpu_custom_call" | custom-call | tf_op jit(solution)/shard_map/pallas_call | solution.py:248
  228.9 0.6 copy.9
  229.5 0.6 copy.10
Async XLA Ops:
  0.6 1.9 copy-start
  2.5 1.0 copy-start.1
  3.6 1.0 copy-start.2
  4.6 0.9 copy-start.3
  5.5 0.9 copy-start.4
